TPU v7x, 32 devices: a whole 2x2x4 slice. The times are simulated.
32 devices in a mesh: seq: 32 (over z, y, x, core), dp: 1.
Axes of the slice: x: 2, y: 2, z: 4, core: 2. Of those that a mesh axis runs over, the one named last changes fastest.
Arguments:
- tokens: bfloat16 [1, 16384, 1536], P('dp', 'seq'), may hold values from -6 to 6
- cotangent: bfloat16 [1, 16384, 1536], P('dp', 'seq'), may hold values from -6 to 6
- conv_weight: float32 [3, 1536], replicated, may hold values from -3.5 to 3.5
- gate_weight: bfloat16 [1536, 1536], P('seq'), may hold values from -0.15625 to 0.15625
- leading_block_factor: bfloat16 [128, 128, 128], P('seq'), may hold values from -0.5 to 0.5
- trailing_block_factor: bfloat16 [128, 128, 128], P('seq'), may hold values from -0.5 to 0.5
Outputs:
- mixed: bfloat16 [1, 16384, 1536], P('dp', 'seq')
- grad_tokens: bfloat16 [1, 16384, 1536], P('dp', 'seq')
- grad_conv: float32 [3, 1536], replicated
- grad_gate: float32 [1536, 1536], P('seq')
- grad_first: float32 [128, 128, 128], P('seq')
- trailing_factor_gradient: float32 [128, 128, 128], P('seq')
All inputs are finite; a program needn't handle non-finite values.
Results may differ from a plain program's by a relative error of at most 0.0067.
Values may be sent and summed in bfloat16 or wider, within the bound.
A program may use at most 128 MiB of HBM per device.

v0:
```python
import jax
import jax.numpy as jnp
from jax import lax
from jax.sharding import PartitionSpec as P


def with_halo(array, sides, width):
    for axis, dim in sides:
        count, length = (lax.axis_size(axis), array.shape[dim])
        up = [(i, (i + 1) % count) for i in range(count - 1)]
        down = [(j, i) for i, j in up]
        last = lax.slice_in_dim(array, length - width, length, axis=dim)
        first = lax.slice_in_dim(array, 0, width, axis=dim)
        before = lax.ppermute(last, axis, up)
        after = lax.ppermute(first, axis, down)
        array = jnp.concatenate([before, array, after], axis=dim)
    return array


def extend(values):
    return with_halo(values, (("seq", 0),), 1)


def regroup(values):
    return lax.all_to_all(values, "seq", split_axis=0, concat_axis=1, tiled=True)


def shards(
    tokens, cotangent, conv_weight, gate_weight, leading_block_factor, trailing_block_factor
):
    features = tokens[0]
    grad_out = cotangent[0]
    tok_rows = features.shape[0]
    feat_width = features.shape[1]
    local_blocks = leading_block_factor.shape[0]
    block_size = leading_block_factor.shape[1]
    feat_wide = features.astype(jnp.float32)
    pad_feat = extend(features).astype(jnp.float32)
    conv_in = (
        conv_weight[0] * pad_feat[:-2] + conv_weight[1] * feat_wide + conv_weight[2] * pad_feat[2:]
    ).astype(jnp.bfloat16)
    convolution_block_list = conv_in.reshape(local_blocks, block_size, feat_width)
    leading_output = jnp.einsum(
        "shz,szy->hsy",
        leading_block_factor,
        convolution_block_list,
        preferred_element_type=jnp.float32,
    ).astype(jnp.bfloat16)
    column_layout = regroup(leading_output)
    trailing_output = jnp.einsum(
        "vpn,vnu->pvu", trailing_block_factor, column_layout, preferred_element_type=jnp.float32
    ).astype(jnp.bfloat16)
    monarch = regroup(trailing_output).reshape(tok_rows, feat_width)
    whole_gate = lax.all_gather(gate_weight, "seq", axis=0, tiled=True)
    gate_act = jnp.dot(features, whole_gate, preferred_element_type=jnp.float32)
    mon_wide = monarch.astype(jnp.float32)
    grad_wide = grad_out.astype(jnp.float32)
    mixed = (mon_wide * gate_act).astype(jnp.bfloat16)
    d_monarch = (grad_wide * gate_act).astype(jnp.bfloat16)
    d_gate = (grad_wide * mon_wide).astype(jnp.bfloat16)
    second_factor_delta = lax.all_to_all(
        d_monarch.reshape(local_blocks, block_size, feat_width),
        "seq",
        split_axis=1,
        concat_axis=0,
        tiled=True,
    )
    d_inner = jnp.einsum(
        "ica,cid->aid",
        trailing_block_factor,
        second_factor_delta,
        preferred_element_type=jnp.float32,
    ).astype(jnp.bfloat16)
    trailing_factor_gradient = jnp.einsum(
        "wxn,xon->xwo", second_factor_delta, column_layout, preferred_element_type=jnp.float32
    )
    d_first = regroup(d_inner)
    d_conv = (
        jnp.einsum(
            "aib,aid->abd", leading_block_factor, d_first, preferred_element_type=jnp.float32
        )
        .astype(jnp.bfloat16)
        .reshape(tok_rows, feat_width)
    )
    grad_first = jnp.einsum(
        "aid,abd->aib", d_first, convolution_block_list, preferred_element_type=jnp.float32
    )
    d_convw = d_conv.astype(jnp.float32)
    conv_part = jnp.stack(
        [
            jnp.sum(d_convw * pad_feat[:-2], axis=0),
            jnp.sum(d_convw * feat_wide, axis=0),
            jnp.sum(d_convw * pad_feat[2:], axis=0),
        ]
    )
    pad_grad = extend(d_conv).astype(jnp.float32)
    conv_back = (
        conv_weight[0] * pad_grad[2:] + conv_weight[1] * d_convw + conv_weight[2] * pad_grad[:-2]
    )
    gate_back = lax.dot_general(
        d_gate, whole_gate, (((1,), (1,)), ((), ())), preferred_element_type=jnp.float32
    )
    grad_tokens = (conv_back + gate_back).astype(jnp.bfloat16)
    weight_part = lax.psum_scatter(
        lax.dot_general(
            features, d_gate, (((0,), (0,)), ((), ())), preferred_element_type=jnp.float32
        ),
        "seq",
        scatter_dimension=0,
        tiled=True,
    )
    grad_first, trailing_factor_gradient = lax.psum((grad_first, trailing_factor_gradient), "dp")
    grad_gate = lax.psum(weight_part, "dp")
    grad_conv = lax.psum(conv_part, ("seq", "dp"))
    return (
        mixed[None],
        grad_tokens[None],
        grad_conv,
        grad_gate,
        grad_first,
        trailing_factor_gradient,
    )


def solution(mesh):
    return jax.shard_map(
        shards,
        mesh=mesh,
        in_specs=(
            P("dp", "seq", None),
            P("dp", "seq", None),
            P(),
            P("seq", None),
            P("seq", None, None),
            P("seq", None, None),
        ),
        out_specs=(
            P("dp", "seq", None),
            P("dp", "seq", None),
            P(),
            P("seq", None),
            P("seq", None, None),
            P("seq", None, None),
        ),
        check_vma=False,
    )
```

profile of v0, /device:TPU:0, one launch (start us, length us, event | category | flops | bytes accessed | tf_op | source)
XLA Modules:
  0.0 438.3 jit_solution(12370799957174921802)
XLA Ops:
  7.9 69.4 %all-gather.2.cloned.1.call-done = bf16[1536,1536]{1,0:T(8,128)(2,1)} async-done(((bf16[48,1536]{1,0:T(8,128)(2,1)}), bf16[1536,1536]{1,0:T(8,128)(2,1)}) %all-gather.2.cloned.1.call-update) | async-done | bytes 4718608 | tf_op jit(solution)/shard_map/all_gather | solution.py:54
  77.3 7.6 %fusion.2 = (bf16[512,1536]{1,0:T(8,128)(2,1)S(1)}, f32[512,1536]{1,0:T(8,128)}) fusion(bf16[1,512,1536]{2,1,0:T(8,128)(2,1)} %param.7, bf16[1536,1536]{1,0:T(8,128)(2,1)} %all-gather.2.cloned.1.call-done, bf16[1,512,1536]{2,1,0:T(8,128)(2,1)} %param.6), kind=kOutput, calls=%fused_computation.9 | convolution fusion | flops 2418278400 | bytes 12582912 | tf_op jit(solution)/shard_map/dot_general | solution.py:55
  86.1 41.2 %all_to_all.63 = bf16[4,128,1536]{2,0,1:T(4,128)(2,1)S(1)} all-to-all(bf16[4,128,1536]{2,0,1:T(4,128)(2,1)S(1)} %copy.58), channel_id=1, replica_groups=mesh['seq'=32,'dp'=1] {'seq'}, dimensions={1} | all-to-all | bytes 3145728 | tf_op jit(solution)/shard_map/all_to_all | solution.py:61
  130.0 2.5 copy.61
  132.5 3.5 all-to-all-start.3
  136.8 2.0 collective-permute-start
  140.2 2.8 collective-permute-done.1
  143.0 1.9 maximum_convert_fusion
  144.9 28.9 %all-to-all-done.3 = bf16[128,4,1536]{2,1,0:T(4,128)(2,1)} async-done(((bf16[128,4,1536]{2,1,0:T(4,128)(2,1)}), bf16[128,4,1536]{2,1,0:T(4,128)(2,1)}, u32[]{:S(2)}, u32[]{:S(2)}) %all-to-all-start.3) | async-done | bytes 1572896 | tf_op jit(solution)/shard_map/all_to_all | solution.py:25
  173.8 3.1 copy.62
  176.9 3.7 all_to_all.58
  180.6 2.6 fusion.9
  188.1 42.4 %all_to_all.64 = bf16[128,4,1536]{2,1,0:T(4,128)(2,1)S(1)} all-to-all(bf16[128,4,1536]{2,1,0:T(4,128)(2,1)S(1)} %copy.53), channel_id=1, replica_groups=mesh['seq'=32,'dp'=1] {'seq'}, dimensions={0} | all-to-all | bytes 3145728 | tf_op jit(solution)/shard_map/all_to_all | solution.py:25
  234.5 40.9 %all_to_all.65 = bf16[128,4,1536]{2,1,0:T(4,128)(2,1)S(1)} all-to-all(bf16[128,4,1536]{2,1,0:T(4,128)(2,1)S(1)} %copy.56), channel_id=1, replica_groups=mesh['seq'=32,'dp'=1] {'seq'}, dimensions={0} | all-to-all | bytes 3145728 | tf_op jit(solution)/shard_map/all_to_all | solution.py:25
  276.2 2.3 reshape.55
  278.4 9.2 %convolution_bitcast_fusion = f32[1536,1536]{0,1:T(8,128)} fusion(f32[1,512,1536]{2,1,0:T(8,128)} %reshape.55, bf16[1,512,1536]{2,1,0:T(8,128)(2,1)} %param.7, bf16[1,512,1536]{2,1,0:T(8,128)(2,1)} %param.6), kind=kOutput, calls=%fused_computation | convolution fusion | flops 2418278400 | bytes 15728640 | tf_op jit(solution)/shard_map/dot_general | solution.py:105
  287.6 9.6 %copy.70 = f32[1536,1536]{1,0:T(8,128)} copy(f32[1536,1536]{0,1:T(8,128)} %convolution_bitcast_fusion) | data formatting | bytes 18874368
  301.2 3.2 fusion.28
  304.4 43.8 %psum.6 = f32[3,1536]{1,0:T(4,128)} all-reduce(f32[3,1536]{1,0:T(4,128)S(1)} %pad_maximum_fusion), channel_id=1, replica_groups=mesh['seq'=32,'dp'=1] {'seq','dp'}, use_global_device_ids=true, to_apply=%region_3.0 | all-reduce | flops 4608 | bytes 36864 | tf_op jit(solution)/shard_map/psum | solution.py:114
  348.3 3.7 maximum_convert_fusion.1
  353.3 2.2 reshape.52
  355.5 4.6 %fusion.15 = bf16[1,512,1536]{2,1,0:T(8,128)(2,1)} fusion(f32[512,1536]{1,0:T(8,128)} %reshape.52, f32[512,1536]{1,0:T(8,128)} %get-tuple-element.41), kind=kLoop, calls=%fused_computation.34 | loop fusion | flops 1572864 | bytes 7864320 | tf_op jit(solution)/shard_map/broadcast_in_dim | solution.py:116
  360.9 7.5 %fusion.14 = bf16[1,512,1536]{2,1,0:T(8,128)(2,1)} fusion(bf16[1536,1536]{1,0:T(8,128)(2,1)} %all-gather.2.cloned.1.call-done, f32[514,1536]{1,0:T(8,128)} %maximum_convert_fusion.1, bf16[512,1536]{1,0:T(8,128)(2,1)S(1)} %bitcast.78, f32[512,1536]{1,0:T(8,128)S(1)} %copy-done.6, bf16[1,512,1536]{2,1,0:T(8,128)(2,1)S(1)} %copy-done.11, ...), kind=kOutput, calls=%fused_computation.31 | convolution fusion | flops 2424569856 | bytes 18892800 | tf_op jit(solution)/shard_map/dot_general | solution.py:100
  368.4 63.1 %reduce-scatter.4.cloned.1.call-done = f32[48,1536]{1,0:T(8,128)} async-done(((f32[1536,1536]{1,0:T(8,128)}), f32[48,1536]{1,0:T(8,128)}) %reduce-scatter.4.cloned.1.call-update) | async-done | bytes 294928
  (57 shorter events, 22.2 us)
Async XLA Ops:
  7.2 173.5 %copy-start = (bf16[4,128,128]{2,1,0:T(8,128)(2,1)S(1)}, bf16[4,128,128]{2,1,0:T(8,128)(2,1)}, u32[]{:S(2)}) copy-start(bf16[4,128,128]{2,1,0:T(8,128)(2,1)} %param.10) | copy-start | bytes 393220
  7.2 70.1 %all-gather.2.cloned.1.call-start = ((), (), s32[]{:S(2)}) async-start(), calls=%async_computation.5 | async-start | bytes 4866048 | tf_op jit(solution)/shard_map/all_gather | solution.py:54
  127.3 1.9 copy-start.12
  128.1 1.1 copy-start.7
  132.5 7.6 %copy-start.13 = (f32[3,1536]{1,0:T(4,128)S(1)}, f32[3,1536]{1,0:T(4,128)}, u32[]{:S(2)}) copy-start(f32[3,1536]{1,0:T(4,128)} %param.8) | copy-start | bytes 55300
  132.5 41.4 %all-to-all-start.3 = ((bf16[128,4,1536]{2,1,0:T(4,128)(2,1)}), bf16[128,4,1536]{2,1,0:T(4,128)(2,1)}, u32[]{:S(2)}, u32[]{:S(2)}) async-start(bf16[128,4,1536]{2,1,0:T(4,128)(2,1)} %copy.61), calls=%async_computation.3 | async-start | bytes 3145728 | tf_op jit(solution)/shard_map/all_to_all | solution.py:25
  136.0 295.5 %reduce-scatter.4.cloned.1.call-start = ((), (), s32[]{:S(2)}) async-start(), calls=%async_computation.6 | async-start | bytes 9732096
  136.8 3.3 collective-permute-start
  138.8 4.2 collective-permute-start.1
  180.6 2.6 copy-start.2
  183.3 1.6 copy-start.3
  184.9 1.1 copy-start.5
  231.2 1.2 copy-start.9
  298.1 50.2 %collective-permute-start.2 = (bf16[1,1536]{1,0:T(2,128)(2,1)S(1)}, bf16[1,1536]{1,0:T(2,128)(2,1)S(1)}, u32[]{:S(2)}, u32[]{:S(2)}) collective-permute-start(bf16[1,1536]{1,0:T(2,128)(2,1)S(1)} %get-tuple-element.36), channel_id=1, source_target_pairs={{0,1},{1,2},{2,3},{3,4},{4,5},{5,6},{6,7},{7,8},{8,9},{9,10},{10,1... | collective-permute-start | bytes 9224 | tf_op jit(solution)/shard_map/ppermute | solution.py:14
  299.9 48.4 %collective-permute-start.3 = (bf16[1,1536]{1,0:T(2,128)(2,1)S(1)}, bf16[1,1536]{1,0:T(2,128)(2,1)S(1)}, u32[]{:S(2)}, u32[]{:S(2)}) collective-permute-start(bf16[1,1536]{1,0:T(2,128)(2,1)S(1)} %get-tuple-element.37), channel_id=1, source_target_pairs={{1,0},{2,1},{3,2},{4,3},{5,4},{6,5},{7,6},{8,7},{9,8},{10,9},{11,1... | collective-permute-start | bytes 9224 | tf_op jit(solution)/shard_map/ppermute | solution.py:15
  348.3 3.8 copy-start.8
  348.3 3.8 copy-start.10
  355.5 4.6 %copy-start.4 = (bf16[4,1536,128]{1,2,0:T(8,128)(2,1)S(1)}, bf16[4,1536,128]{1,2,0:T(8,128)(2,1)}, u32[]{:S(2)}) copy-start(bf16[4,1536,128]{1,2,0:T(8,128)(2,1)} %copy-done.3) | copy-start | bytes 4718596
  355.5 4.6 %copy-start.6 = (f32[512,1536]{1,0:T(8,128)S(1)}, f32[512,1536]{1,0:T(8,128)}, u32[]{:S(2)}) copy-start(f32[512,1536]{1,0:T(8,128)} %reshape.52) | copy-start | bytes 9437188
  355.5 5.3 %copy-start.11 = (bf16[1,512,1536]{2,1,0:T(8,128)(2,1)S(1)}, bf16[1,512,1536]{2,1,0:T(8,128)(2,1)}, u32[]{:S(2)}) copy-start(bf16[1,512,1536]{2,1,0:T(8,128)(2,1)} %param.7) | copy-start | bytes 4718596
  360.9 70.6 %copy-start.1 = (bf16[4,128,128]{2,1,0:T(8,128)(2,1)S(1)}, bf16[4,128,128]{2,1,0:T(8,128)(2,1)}, u32[]{:S(2)}) copy-start(bf16[4,128,128]{2,1,0:T(8,128)(2,1)} %param.10) | copy-start | bytes 393220
Sparse Core Ops, SparseCore 0:
  10.9 66.3 all-gather.1
  297.4 134.0 reduce-scatter.3
where the time goes:
time: 439 us; the launch traced here: 438 us
  blocking collectives  168 us (38%)
  waiting for transfers between devices  165 us (38%)
  local copies, waits for them, and re-layouts  34.9 us (8%)
  matrix products  33.6 us (8%)
  between operations  14.3 us (3%)
  other arithmetic  12.3 us (3%)
  starting transfers between devices  9.97 us (2%)
    all_to_all x2, blocking collectives, regroup(): lax.all_to_all(values, 'seq', split_axis=0, concat_axis=1, tiled=True)  83.3 us
    all_gather x1, waiting for transfers between devices, shards(): whole_gate = lax.all_gather(gate_weight, 'seq', axis=0, tiled=True)  69.4 us
    unnamed x3, waiting for transfers between devices  63.8 us
    psum x1, blocking collectives, shards(): grad_conv = lax.psum(conv_part, ('seq', 'dp'))  43.8 us
    all_to_all x1, blocking collectives, shards(): lax.all_to_all(d_monarch.reshape(local_blocks, block_size, feat_width), '...  41.2 us
    all_to_all x1, waiting for transfers between devices, regroup(): lax.all_to_all(values, 'seq', split_axis=0, concat_axis=1, tiled=True)  28.9 us
    unnamed x29, local copies, waits for them, and re-layouts  13.9 us
    dot_general x1, matrix products, shards(): lax.dot_general(features, d_gate, (((0,), (0,)), ((), ())), preferred_ele...  9.16 us
  transfers between devices with their start and end apart: 7, of which 4 were waited for; matrix products, arithmetic and copies ran while one was open for 6% of the time, Pallas kernels for 0%

commit v1 on v0

v1 whole, which is shorter than its diff:
```python
import functools

import jax
import jax.numpy as jnp
from jax import lax
from jax.experimental import pallas as pl
from jax.experimental.pallas import tpu as pltpu
from jax.sharding import PartitionSpec as P

MESH = pl.DeviceIdType.MESH
BF = jnp.bfloat16
F32 = jnp.float32
CHUNKS = 3
LIMIT = 52 * 1024 * 1024


def mm(a, b):
    return jnp.dot(a, b, preferred_element_type=F32)


def mm_t(a, b):
    return lax.dot_general(a, b, (((1,), (1,)), ((), ())), preferred_element_type=F32)


def iotas(rows, columns):
    shape = (rows, columns)
    return lax.broadcasted_iota(jnp.int32, shape, 0), lax.broadcasted_iota(jnp.int32, shape, 1)


def one_hot(mask):
    return jnp.where(mask, 1.0, 0.0).astype(BF)


def natural_order(rows, blocks, per, transposed=False):
    out, src = iotas(rows, rows)
    if transposed:
        out, src = src, out
    size = rows // blocks
    block, rest = out // size, out % size
    owner, inner = rest // per, rest % per
    return one_hot(src == owner * (blocks * per) + block * per + inner)


def inner_first(rows, per, transposed=False):
    out, src = iotas(rows, rows)
    if transposed:
        out, src = src, out
    size = rows // per
    return one_hot(src == (out % size) * per + out // size)


def greet(me, n):
    barrier = pltpu.get_barrier_semaphore()

    def body(t, carry):
        peer = lax.rem(me + t, n)
        pl.semaphore_signal(barrier, inc=1, device_id={"seq": peer}, device_id_type=MESH)
        return carry

    lax.fori_loop(1, n, body, 0)
    pl.semaphore_wait(barrier, n - 1)


def spread(me, n, k, src, dst, send_sem, recv_sem, piece):
    def body(t, carry):
        peer = lax.rem(me + lax.rem(t * 11, n), n)
        pltpu.make_async_remote_copy(
            src_ref=src.at[k, pl.ds(pl.multiple_of(peer * piece, piece), piece)],
            dst_ref=dst.at[k, pl.ds(pl.multiple_of(me * piece, piece), piece)],
            send_sem=send_sem.at[k],
            recv_sem=recv_sem.at[k],
            device_id={"seq": peer},
            device_id_type=MESH,
        ).start()
        return carry

    lax.fori_loop(1, n, body, 0)
    own = pl.ds(pl.multiple_of(me * piece, piece), piece)
    dst[k, own, :] = src[k, own, :]


def settle(ref, sem):
    pltpu.make_async_copy(ref, ref, sem).wait()


def shifted(x, before, after):
    rows = x.shape[0]
    at = lax.broadcasted_iota(jnp.int32, x.shape, 0)
    prev = jnp.where(at == 0, before, pltpu.roll(x, 1, 0))
    nxt = jnp.where(at == rows - 1, after, pltpu.roll(x, rows - 1, 0))
    return prev, nxt


def forward(
    n, tok, taps, lead, trail,
    conv, cols, mon, lead_t, trail_t, halo,
    hbuf, sa, ra, sb, rb, lead_m, trail_m, hs, hr, a_s, a_r, b_s, b_r,
):
    me = lax.axis_index("seq")
    right, left = lax.rem(me + 1, n), lax.rem(me + n - 1, n)
    rows, width = tok.shape
    blocks = lead.shape[0]
    size = lead.shape[1]
    per = size // n
    piece = blocks * per
    cw = width // CHUNKS
    greet(me, n)
    to_right = pltpu.make_async_remote_copy(
        src_ref=tok.at[pl.ds(rows - 16, 16)], dst_ref=hbuf.at[0], send_sem=hs.at[0],
        recv_sem=hr.at[0], device_id={"seq": right}, device_id_type=MESH)
    to_left = pltpu.make_async_remote_copy(
        src_ref=tok.at[pl.ds(0, 16)], dst_ref=hbuf.at[1], send_sem=hs.at[1],
        recv_sem=hr.at[1], device_id={"seq": left}, device_id_type=MESH)
    to_right.start()
    to_left.start()
    r, c = iotas(rows, rows)
    flat = jnp.concatenate([lead[a] for a in range(blocks)], axis=0)
    turned = mm(natural_order(rows, blocks, per, True), flat).astype(BF)
    wide = jnp.concatenate([turned] * blocks, axis=1)
    lead_m[...] = jnp.where((r // per) % blocks == c // size, wide, jnp.zeros_like(wide))
    to_right.wait()
    to_left.wait()
    zero = jnp.zeros((16, width), BF)
    halo[0] = jnp.where(me == 0, zero, hbuf[0])
    halo[1] = jnp.where(me == n - 1, zero, hbuf[1])
    for k in range(CHUNKS):
        at = pl.ds(k * cw, cw)
        x = tok[:, at].astype(F32)
        prev, nxt = shifted(x, halo[0, :, at].astype(F32)[15:16], halo[1, :, at].astype(F32)[0:1])
        conv[k] = (taps[0:1, at] * prev + taps[1:2, at] * x + taps[2:3, at] * nxt).astype(BF)
        sa[k] = mm(lead_m[...], conv[k]).astype(BF)
        spread(me, n, k, sa, ra, a_s, a_r, piece)
    flat = jnp.concatenate([trail[j] for j in range(per)], axis=0)
    turned = mm(inner_first(rows, per, True), flat).astype(BF)
    er, ec = iotas(size, rows)
    wide = mm(turned, one_hot(ec // per == er)).astype(BF)
    trail_m[...] = jnp.where(r % per == c % per, wide, jnp.zeros_like(wide))
    trail_t[...] = trail_m[...].T
    lead_t[...] = lead_m[...].T
    others = (n - 1) * piece
    for k in range(CHUNKS):
        settle(ra.at[k, pl.ds(0, others)], a_r.at[k])
        sb[k] = mm(trail_m[...], ra[k]).astype(BF)
        spread(me, n, k, sb, rb, b_s, b_r, piece)
        cols[k] = ra[k]
    order = natural_order(rows, blocks, per)
    for k in range(CHUNKS):
        settle(rb.at[k, pl.ds(0, others)], b_r.at[k])
        mon[k] = mm(order, rb[k]).astype(BF)
    for k in range(CHUNKS):
        settle(sa.at[k, pl.ds(0, others)], a_s.at[k])
        settle(sb.at[k, pl.ds(0, others)], b_s.at[k])


def middle(blocks, per, tok, tok_b, cot, mon, w, mixed, d_gate, send_c, part, tok_t):
    del tok_b
    rows = tok.shape[0]

    @pl.when(pl.program_id(0) == 0)
    def _():
        tok_t[...] = tok[...].T

    gate = mm(tok[...], w[...])
    m = mon[0].astype(F32)
    g = cot[...].astype(F32)
    mixed[...] = (m * gate).astype(BF)
    dg = (g * m).astype(BF)
    d_gate[...] = dg
    send_c[0] = mm(natural_order(rows, blocks, per, True), (g * gate).astype(BF)).astype(BF)
    part[...] = mm(tok_t[...], dg)


def backward(
    n, blocks, per, group, send_c, cols, trail_t, lead_t, tok, halo, conv, d_gate, w, taps,
    g_tok, g_conv, g_first, g_trail,
    rc, sd, rd, dcv, gb, hbuf, cp, p1, s2, p2, qcols,
    c_s, c_r, d_s, d_r, hs, hr, p_s, p_r, z_s, z_r,
):
    me = lax.axis_index("seq")
    right, left = lax.rem(me + 1, n), lax.rem(me + n - 1, n)
    rows, width = tok.shape
    size = rows // blocks
    piece = blocks * per
    cw = width // CHUNKS
    others = (n - 1) * piece
    teams = n // group
    mine, team = lax.rem(me, group), me // group
    greet(me, n)
    for k in range(CHUNKS):
        spread(me, n, k, send_c, rc, c_s, c_r, piece)
    swap = inner_first(rows, per)
    for k in range(CHUNKS):
        gb[k] = mm_t(d_gate[...], w[k * cw:(k + 1) * cw, :])
        qcols[k] = mm(swap, cols[k]).astype(BF)
    for k in range(CHUNKS):
        settle(rc.at[k, pl.ds(0, others)], c_r.at[k])
        sd[k] = mm(trail_t[...], rc[k]).astype(BF)
        spread(me, n, k, sd, rd, d_s, d_r, piece)
    for k in range(CHUNKS):
        turned = mm(swap, rc[k]).astype(BF)
        for j in range(per):
            at = pl.ds(j * size, size)
            term = mm_t(turned[j * size:(j + 1) * size], qcols[k, at, :])
            g_trail[j] = term if k == 0 else g_trail[j] + term
    order = natural_order(rows, blocks, per)
    for k in range(CHUNKS):
        at = pl.ds(k * cw, cw)
        settle(rd.at[k, pl.ds(0, others)], d_r.at[k])
        d = mm(lead_t[...], rd[k]).astype(BF)
        dcv[k] = d
        for side, (first, peer) in enumerate(((rows - 16, right), (0, left))):
            pltpu.make_async_remote_copy(
                src_ref=dcv.at[k, pl.ds(first, 16)], dst_ref=hbuf.at[side, k],
                send_sem=hs.at[side, k], recv_sem=hr.at[side, k],
                device_id={"seq": peer}, device_id_type=MESH).start()
        x = tok[:, at].astype(F32)
        prev, nxt = shifted(x, halo[0, :, at].astype(F32)[15:16], halo[1, :, at].astype(F32)[0:1])
        d = d.astype(F32)
        cp[k] = jnp.concatenate(
            [jnp.sum(d * v, axis=0, keepdims=True) for v in (prev, x, nxt)]
            + [jnp.zeros((5, cw), F32)], axis=0)
        p1[k, mine] = cp[k]
        for t in range(1, group):
            peer = team * group + lax.rem(mine + t, group)
            pltpu.make_async_remote_copy(
                src_ref=cp.at[k], dst_ref=p1.at[k, mine], send_sem=p_s.at[k],
                recv_sem=p_r.at[k], device_id={"seq": peer}, device_id_type=MESH).start()
        turned = mm(order, rd[k]).astype(BF)
        for a in range(blocks):
            term = mm_t(turned[a * size:(a + 1) * size], conv[k, pl.ds(a * size, size), :])
            g_first[a] = term if k == 0 else g_first[a] + term
    for k in range(CHUNKS):
        settle(p1.at[k, pl.ds(0, group - 1)], p_r.at[k])
        total = p1[k, 0]
        for t in range(1, group):
            total = total + p1[k, t]
        s2[k] = total
        p2[k, team] = total
        for t in range(1, teams):
            peer = lax.rem(me + t * group, n)
            pltpu.make_async_remote_copy(
                src_ref=s2.at[k], dst_ref=p2.at[k, team], send_sem=z_s.at[k],
                recv_sem=z_r.at[k], device_id={"seq": peer}, device_id_type=MESH).start()
    for k in range(CHUNKS):
        at = pl.ds(k * cw, cw)
        for side in range(2):
            settle(hbuf.at[side, k], hr.at[side, k])
        before = hbuf[0, k].astype(F32)[15:16]
        after = hbuf[1, k].astype(F32)[0:1]
        before = jnp.where(me == 0, jnp.zeros_like(before), before)
        after = jnp.where(me == n - 1, jnp.zeros_like(after), after)
        d = dcv[k].astype(F32)
        prev, nxt = shifted(d, before, after)
        back = taps[0:1, at] * nxt + taps[1:2, at] * d + taps[2:3, at] * prev
        g_tok[:, at] = (back + gb[k]).astype(BF)
    for k in range(CHUNKS):
        settle(p2.at[k, pl.ds(0, teams - 1)], z_r.at[k])
        total = p2[k, 0]
        for t in range(1, teams):
            total = total + p2[k, t]
        g_conv[:, pl.ds(k * cw, cw)] = total
    for k in range(CHUNKS):
        settle(send_c.at[k, pl.ds(0, others)], c_s.at[k])
        settle(sd.at[k, pl.ds(0, others)], d_s.at[k])
        settle(p1.at[k, pl.ds(0, group - 1)], p_s.at[k])
        settle(p2.at[k, pl.ds(0, teams - 1)], z_s.at[k])
        for side in range(2):
            settle(hbuf.at[side, k], hs.at[side, k])


def shards(n, tokens, cotangent, taps, gate_weight, lead, trail):
    features, grad_out = tokens[0], cotangent[0]
    rows, width = features.shape
    blocks, size = lead.shape[0], lead.shape[1]
    per = size // n
    cw = width // CHUNKS
    group = 8 if n % 8 == 0 and n > 8 else n // 2
    sds = jax.ShapeDtypeStruct
    vmem = pl.BlockSpec(memory_space=pltpu.VMEM)
    dma = pltpu.SemaphoreType.DMA
    stack = (CHUNKS, rows, cw)
    square = (rows, rows)
    block = pltpu.VMEM(stack, BF)

    whole_gate = lax.all_gather(gate_weight, "seq", axis=0, tiled=True)

    conv, cols, mon, lead_t, trail_t, halo = pl.pallas_call(
        functools.partial(forward, n),
        out_shape=[sds(stack, BF), sds(stack, BF), sds(stack, BF), sds(square, BF),
                   sds(square, BF), sds((2, 16, width), BF)],
        in_specs=[vmem] * 4,
        out_specs=[vmem] * 6,
        scratch_shapes=[pltpu.VMEM((2, 16, width), BF), block, block, block, block,
                        pltpu.VMEM(square, BF), pltpu.VMEM(square, BF), dma((2,)), dma((2,)),
                        dma((CHUNKS,)), dma((CHUNKS,)), dma((CHUNKS,)), dma((CHUNKS,))],
        compiler_params=pltpu.CompilerParams(
            collective_id=0, has_side_effects=True, vmem_limit_bytes=LIMIT),
        cost_estimate=pl.CostEstimate(
            flops=6 * rows * rows * width, bytes_accessed=200_000_000, transcendentals=0),
        name="forward_exchange",
    )(features, taps, lead, trail)

    whole_gate, mon = lax.optimization_barrier((whole_gate, mon))

    whole = pl.BlockSpec((rows, width), lambda k: (0, 0))
    strip = pl.BlockSpec((rows, cw), lambda k: (0, k))
    layer = pl.BlockSpec((1, rows, cw), lambda k: (k, 0, 0))
    tall = pl.BlockSpec((width, cw), lambda k: (0, k))
    mixed, d_gate, send_c, part = pl.pallas_call(
        functools.partial(middle, blocks, per),
        grid=(CHUNKS,),
        out_shape=[sds((rows, width), BF), sds((rows, width), BF), sds(stack, BF),
                   sds((width, width), F32)],
        in_specs=[whole, strip, strip, layer, tall],
        out_specs=[strip, strip, layer, tall],
        scratch_shapes=[pltpu.VMEM((width, rows), BF)],
        compiler_params=pltpu.CompilerParams(vmem_limit_bytes=LIMIT),
        cost_estimate=pl.CostEstimate(
            flops=4 * rows * width * width, bytes_accessed=24_000_000, transcendentals=0),
        name="gate_and_weight",
    )(features, features, grad_out, mon, whole_gate)

    part, send_c = lax.optimization_barrier((part, send_c))
    grad_gate = lax.psum_scatter(part, "seq", scatter_dimension=0, tiled=True)

    grad_tokens, grad_conv, grad_first, grad_trail = pl.pallas_call(
        functools.partial(backward, n, blocks, per, group),
        out_shape=[sds((rows, width), BF), sds((8, width), F32), sds(lead.shape, F32),
                   sds(trail.shape, F32)],
        in_specs=[vmem] * 10,
        out_specs=[vmem] * 4,
        scratch_shapes=[block, block, block, block, pltpu.VMEM(stack, F32),
                        pltpu.VMEM((2, CHUNKS, 16, cw), BF),
                        pltpu.VMEM((CHUNKS, 8, cw), F32),
                        pltpu.VMEM((CHUNKS, group, 8, cw), F32),
                        pltpu.VMEM((CHUNKS, 8, cw), F32),
                        pltpu.VMEM((CHUNKS, n // group, 8, cw), F32), block]
        + [dma((CHUNKS,))] * 4 + [dma((2, CHUNKS))] * 2 + [dma((CHUNKS,))] * 4,
        compiler_params=pltpu.CompilerParams(
            collective_id=1, has_side_effects=True, vmem_limit_bytes=LIMIT),
        cost_estimate=pl.CostEstimate(
            flops=6 * rows * rows * width, bytes_accessed=200_000_000, transcendentals=0),
        name="backward_exchange",
    )(send_c, cols, trail_t, lead_t, features, halo, conv, d_gate, whole_gate, taps)

    grad_conv, grad_gate, grad_first, grad_trail = lax.psum(
        (grad_conv[:3], grad_gate, grad_first, grad_trail), "dp")
    return mixed[None], grad_tokens[None], grad_conv, grad_gate, grad_first, grad_trail


def solution(mesh):
    seq = P("dp", "seq", None)
    specs = (seq, seq, P(), P("seq", None), P("seq", None, None), P("seq", None, None))
    return jax.shard_map(
        functools.partial(shards, mesh.shape["seq"]),
        mesh=mesh,
        in_specs=specs,
        out_specs=specs,
        check_vma=False,
    )
```

time: 439 us -> 299 us (0.68)
  Pallas kernels: 0 us -> 232 us
  blocking collectives: 168 us -> 0 us
  waiting for transfers between devices: 165 us -> 43.5 us
  matrix products: 33.6 us -> 0 us
  local copies, waits for them, and re-layouts: 34.9 us -> 9.09 us
  other arithmetic: 12.3 us -> 0 us
  starting transfers between devices: 9.97 us -> 0.08 us
    pallas_call x0 -> x3, Pallas kernels: none -> 232 us  [the longest x1 113 us: shards(): pl.pallas_call(functools.partial(backward, n, blocks, per, group), out_sh...]
    all_to_all x3 -> x0, blocking collectives: 124 us -> none  [the longest x2 83.3 us: regroup(): lax.all_to_all(values, 'seq', split_axis=0, concat_axis=1, tiled=True)]
    all_gather x1, waiting for transfers between devices: 69.4 us -> 0.02 us  [shards(): whole_gate = lax.all_gather(gate_weight, 'seq', axis=0, tiled=True)]
    unnamed x3 -> x2, waiting for transfers between devices: 63.8 us -> 0.7 us
    psum x1 -> x0, blocking collectives: 43.8 us -> none  [shards(): grad_conv = lax.psum(conv_part, ('seq', 'dp'))]
    reduce_scatter x0 -> x1, waiting for transfers between devices: none -> 42.8 us  [shards(): grad_gate = lax.psum_scatter(part, 'seq', scatter_dimension=0, tiled=True)]
    dot_general x9 -> x0, matrix products: 33.6 us -> none  [the longest x1 9.16 us: shards(): lax.dot_general(features, d_gate, (((0,), (0,)), ((), ())), preferred_ele...]
    all_to_all x1 -> x0, waiting for transfers between devices: 28.9 us -> none  [regroup(): lax.all_to_all(values, 'seq', split_axis=0, concat_axis=1, tiled=True)]
  transfers between devices with their start and end apart: 7 -> 2, of which waited for: 4 -> 1; matrix products, arithmetic and copies ran while one was open for 6% -> 0% of each run, Pallas kernels for 0% -> 73%
where the time goes in v1:
time: 299 us
  Pallas kernels  232 us (78%)
  waiting for transfers between devices  43.5 us (15%)
  between operations  14.1 us (5%)
  local copies, waits for them, and re-layouts  9.09 us (3%)
    pallas_call x1, Pallas kernels, shards(): pl.pallas_call(functools.partial(backward, n, blocks, per, group), out_sh...  113 us
    pallas_call x1, Pallas kernels, shards(): pl.pallas_call(functools.partial(forward, n), out_shape=[sds(stack, BF),...  106 us
    reduce_scatter x1, waiting for transfers between devices, shards(): grad_gate = lax.psum_scatter(part, 'seq', scatter_dimension=0, tiled=True)  42.8 us
    pallas_call x1, Pallas kernels, shards(): pl.pallas_call(functools.partial(middle, blocks, per), grid=(CHUNKS,), ou...  13.6 us
    unnamed x13, local copies, waits for them, and re-layouts  8.48 us
  transfers between devices with their start and end apart: 2, of which 1 were waited for; matrix products, arithmetic and copies ran while one was open for 0% of the time, Pallas kernels for 73%

profile of v1, /device:TPU:0, one launch (start us, length us, event | category | flops | bytes accessed | tf_op | source)
XLA Modules:
  0.0 299.0 jit_solution(9331269427870100997)
XLA Ops:
  7.2 0.0 all-gather.2.cloned.1.call-start
  7.2 0.7 all-gather.2.cloned.1.call-update
  7.9 0.0 reduce-scatter.2.cloned.1.call-start
  7.9 0.0 copy-start.1
  8.0 0.7 copy-done.1
  8.7 0.0 copy-start.3
  8.7 0.9 copy-done.3
  9.6 0.0 copy-start.4
  9.6 0.9 copy-done.4
  10.5 105.8 %forward_exchange.1 = (bf16[3,512,512]{2,1,0:T(8,128)(2,1)}, bf16[3,512,512]{2,1,0:T(8,128)(2,1)}, bf16[3,512,512]{2,1,0:T(8,128)(2,1)}, bf16[512,512]{1,0:T(8,1...) custom-call(bf16[512,1536]{1,0:T(8,128)(2,1)} %bitcast.4, f32[3,1536]{1,0:T(4,128)S(1)} %copy-done.1, ...), custom_call_target="tpu_custom_call" | custom-call | flops 2415919104 | bytes 200000000 | tf_op jit(solution)/shard_map/forward_exchange/pallas_call | solution.py:287
  116.3 0.0 all-gather.2.cloned.1.call-done.w
  116.3 13.6 %gate_and_weight.1 = (bf16[512,1536]{1,0:T(8,128)(2,1)}, bf16[512,1536]{1,0:T(8,128)(2,1)S(1)}, bf16[3,512,512]{2,1,0:T(8,128)(2,1)}, f32[1536,1536]{1,0:T(8,128)}) custom-call(bf16[512,1536]{1,0:T(8,128)(2,1)} %bitcast.5, bf16[512,1536]{1,0:T(8,128)(2,1)} %bitcast.6, bf16[512,1536]{1,0:T(8,128)(2,1)} %bitcast.9, ...), custom_call_target="tpu_custom_call" | custom-call | flops 4831838208 | bytes 24000000 | tf_op jit(solution)/shard_map/gate_and_weight/pallas_call | solution.py:309
  129.9 0.0 copy-start
  129.9 1.2 copy-done
  131.1 0.0 copy-start.2
  131.1 0.0 reduce-scatter.2.cloned.1.call-update
  131.1 0.7 copy-done.2
  131.8 112.9 %backward_exchange.1 = (bf16[512,1536]{1,0:T(8,128)(2,1)}, f32[8,1536]{1,0:T(8,128)S(1)}, f32[4,128,128]{2,1,0:T(8,128)S(1)}, f32[4,128,128]{2,1,0:T(8,128)S(1)}) custom-call(bf16[3,512,512]{2,1,0:T(8,128)(2,1)} %get-tuple-element.30.send_c, bf16[3,512,512]{2,1,0:T(8,128)(2,1)} %get-tuple-element.31.cols, bf16[512,512]{1,0:T(8,128)(2,1)S(1)} %get-tuple-element.32.trail_t, ...), custom_call_target="tpu_custom_call" | custom-call | flops 2415919104 | bytes 200000000 | tf_op jit(solution)/shard_map/backward_exchange/pallas_call | solution.py:326
  244.7 0.6 slice.3
  245.3 42.8 %reduce-scatter.2.cloned.1.call-done = f32[48,1536]{1,0:T(8,128)} async-done(((f32[1536,1536]{1,0:T(8,128)}), f32[48,1536]{1,0:T(8,128)}) %reduce-scatter.2.cloned.1.call-update) | async-done | bytes 294928 | tf_op jit(solution)/shard_map/reduce_scatter | solution.py:324
  288.1 2.7 copy.15
  290.7 0.7 copy.16
  291.4 0.7 copy.17
Async XLA Ops:
  7.2 109.1 %all-gather.2.cloned.1.call-start = ((), (), s32[]{:S(2)}) async-start(), calls=%async_computation.1 | async-start | bytes 4866048 | tf_op jit(solution)/shard_map/all_gather | solution.py:285
  7.9 280.2 %reduce-scatter.2.cloned.1.call-start = ((), (), s32[]{:S(2)}) async-start(), calls=%async_computation.2 | async-start | bytes 9732096 | tf_op jit(solution)/shard_map/reduce_scatter | solution.py:324
  7.9 0.7 copy-start.1
  8.7 0.9 copy-start.3
  9.6 0.9 copy-start.4
  129.9 1.2 copy-start
  131.1 0.7 copy-start.2
Sparse Core Ops, SparseCore 0:
  10.9 91.7 all-gather.1
  131.2 156.8 reduce-scatter.1

commit v2 on v1

v2 whole, which is shorter than its diff:
```python
import functools

import jax
import jax.numpy as jnp
from jax import lax
from jax.experimental import pallas as pl
from jax.experimental.pallas import tpu as pltpu
from jax.sharding import PartitionSpec as P

MESH = pl.DeviceIdType.MESH
BF = jnp.bfloat16
F32 = jnp.float32
CHUNKS = 2
LIMIT = 60 * 1024 * 1024


def mm(a, b):
    return jnp.dot(a, b, preferred_element_type=F32)


def mm_t(a, b):
    return lax.dot_general(a, b, (((1,), (1,)), ((), ())), preferred_element_type=F32)


def iotas(rows, columns):
    shape = (rows, columns)
    return lax.broadcasted_iota(jnp.int32, shape, 0), lax.broadcasted_iota(jnp.int32, shape, 1)


def one_hot(mask):
    return jnp.where(mask, 1.0, 0.0).astype(BF)


def natural_order(rows, blocks, per, transposed=False):
    out, src = iotas(rows, rows)
    if transposed:
        out, src = src, out
    size = rows // blocks
    block, rest = out // size, out % size
    owner, inner = rest // per, rest % per
    return one_hot(src == owner * (blocks * per) + block * per + inner)


def inner_first(rows, per, transposed=False):
    out, src = iotas(rows, rows)
    if transposed:
        out, src = src, out
    size = rows // per
    return one_hot(src == (out % size) * per + out // size)


def greet(me, n):
    barrier = pltpu.get_barrier_semaphore()

    def body(t, carry):
        peer = lax.rem(me + t, n)
        pl.semaphore_signal(barrier, inc=1, device_id={"seq": peer}, device_id_type=MESH)
        return carry

    lax.fori_loop(1, n, body, 0)
    pl.semaphore_wait(barrier, n - 1)


def spread(me, n, k, src, dst, send_sem, recv_sem, piece):
    def body(t, carry):
        peer = lax.rem(me + lax.rem(t * 11, n), n)
        pltpu.make_async_remote_copy(
            src_ref=src.at[k, pl.ds(pl.multiple_of(peer * piece, piece), piece)],
            dst_ref=dst.at[k, pl.ds(pl.multiple_of(me * piece, piece), piece)],
            send_sem=send_sem.at[k],
            recv_sem=recv_sem.at[k],
            device_id={"seq": peer},
            device_id_type=MESH,
        ).start()
        return carry

    lax.fori_loop(1, n, body, 0)
    own = pl.ds(pl.multiple_of(me * piece, piece), piece)
    dst[k, own, :] = src[k, own, :]


def settle(ref, sem):
    pltpu.make_async_copy(ref, ref, sem).wait()


def shifted(x, before, after):
    rows = x.shape[0]
    at = lax.broadcasted_iota(jnp.int32, x.shape, 0)
    prev = jnp.where(at == 0, before, pltpu.roll(x, 1, 0))
    nxt = jnp.where(at == rows - 1, after, pltpu.roll(x, rows - 1, 0))
    return prev, nxt


def flipped(me, bit):
    return me + (1 - 2 * ((me // bit) % 2)) * bit


def hop(src, dst, send_sem, recv_sem, peer):
    pltpu.make_async_remote_copy(
        src_ref=src, dst_ref=dst, send_sem=send_sem, recv_sem=recv_sem,
        device_id={"seq": peer}, device_id_type=MESH).start()


def each(count, body):
    def step(t, carry):
        body(t)
        return carry

    lax.fori_loop(0, count, step, 0)


def band(index, rows):
    return pl.ds(pl.multiple_of(index * rows, 16), rows)


ORDERS = ((2, 4), (4, 2))


def layer(
    n, tok, cot, taps, gw, lead, trail,
    mixed, g_tok, g_conv, g_gate, g_first, g_trail,
    halo, hbuf, w, part, r1, r2, r3, r4, conv, sa, ra, sb, rb, sc, rc, sd, rd, dcv, dg, gate,
    tok_t, lead_m, lead_t, trail_m, trail_t, cp, p1, s2, p2,
    a_s, a_r, b_s, b_r, c_s, c_r, d_s, d_r, t_s, t_r, hs, hr, p_s, p_r, z_s, z_r,
    w_s, w_r, g_s, g_r,
):
    me = lax.axis_index("seq")
    right, left = lax.rem(me + 1, n), lax.rem(me + n - 1, n)
    rows, width = tok.shape
    blocks, size = lead.shape[0], lead.shape[1]
    per = size // n
    piece = blocks * per
    cw = width // CHUNKS
    others = (n - 1) * piece
    own = width // n
    teams, group = n // 8, 8
    mine, team = lax.rem(me, group), me // group
    core = lax.rem(me, 2)

    def bit_of(bit):
        return (me // bit) % 2

    def gather_teams():
        for h in range(CHUNKS):
            at = pl.ds(h * cw, cw)
            w[h, band(me, own), :] = gw[:, at]
            for t in range(1, teams):
                hop(gw.at[:, at], w.at[h, band(me, own)], w_s.at[h, 0], w_r.at[h, 0],
                    lax.rem(me + t * group, n))

    def gather_step(h, stage):
        first, second = ORDERS[h]
        settle(w.at[h, pl.ds(0, (teams - 1) * own if stage == 1 else (teams << (stage - 2)) * own)],
               w_r.at[h, stage - 1])
        bit = (first, second, 1)[stage - 1]
        spans = 1 << (stage - 1)

        def body(t):
            z, v = t // spans, t % spans
            if stage == 1:
                inner = mine
            elif stage == 2:
                inner = mine - bit_of(first) * first + v * first
            else:
                inner = core + 2 * v
            d = z * group + inner
            hop(w.at[h, band(d, own)], w.at[h, band(d, own)], w_s.at[h, stage],
                w_r.at[h, stage], flipped(me, bit))

        each(teams * spans, body)

    def piece_of(h, stage, t, keep):
        first, second = ORDERS[h]
        if stage == 0:
            return 2 * t + (core if keep else 1 - core)
        mark = bit_of(first)
        if stage == 1:
            z, v = t // 2, t % 2
            return z * group + core + v * second + (mark if keep else 1 - mark) * first
        far = bit_of(second)
        return t * group + core + mark * first + (far if keep else 1 - far) * second

    landing = (r1, r2, r3)

    def scatter_step(h, stage):
        count = n >> (stage + 1)
        peer = flipped(me, (1, *ORDERS[h])[stage])

        def body(t):
            hop(part.at[h, band(piece_of(h, stage, t, False), own)],
                landing[stage].at[h, band(t, own)], g_s.at[h, stage], g_r.at[h, stage], peer)

        each(count, body)

    def scatter_sum(h, stage):
        count = n >> (stage + 1)
        settle(landing[stage].at[h], g_r.at[h, stage])

        def body(t):
            at = band(piece_of(h, stage, t, True), own)
            got = landing[stage][h, band(t, own), :].astype(F32)
            part[h, at, :] = (part[h, at, :].astype(F32) + got).astype(BF)

        each(count, body)

    def scatter_teams(h):
        r4[h, band(team, own), :] = part[h, band(me, own), :]
        for t in range(1, teams):
            peer = lax.rem(me + t * group, n)
            hop(part.at[h, band(peer, own)], r4.at[h, band(team, own)], g_s.at[h, 3],
                g_r.at[h, 3], peer)

    greet(me, n)
    hop(tok.at[pl.ds(rows - 16, 16)], halo.at[0], t_s.at[0], t_r.at[0], right)
    hop(tok.at[pl.ds(0, 16)], halo.at[1], t_s.at[1], t_r.at[1], left)
    gather_teams()
    r, c = iotas(rows, rows)
    flat = jnp.concatenate([lead[a] for a in range(blocks)], axis=0)
    turned = mm(natural_order(rows, blocks, per, True), flat).astype(BF)
    wide = jnp.concatenate([turned] * blocks, axis=1)
    lead_m[...] = jnp.where((r // per) % blocks == c // size, wide, jnp.zeros_like(wide))
    for side in range(2):
        settle(halo.at[side], t_r.at[side])

    def around(k):
        at = pl.ds(k * cw, cw)
        x = tok[:, at].astype(F32)
        before = halo[0, :, at].astype(F32)[15:16]
        after = halo[1, :, at].astype(F32)[0:1]
        before = jnp.where(me == 0, jnp.zeros_like(before), before)
        after = jnp.where(me == n - 1, jnp.zeros_like(after), after)
        prev, nxt = shifted(x, before, after)
        return prev, x, nxt

    for k in range(CHUNKS):
        at = pl.ds(k * cw, cw)
        prev, x, nxt = around(k)
        conv[k] = (taps[0:1, at] * prev + taps[1:2, at] * x + taps[2:3, at] * nxt).astype(BF)
        sa[k] = mm(lead_m[...], conv[k]).astype(BF)
        spread(me, n, k, sa, ra, a_s, a_r, piece)
    flat = jnp.concatenate([trail[j] for j in range(per)], axis=0)
    turned = mm(inner_first(rows, per, True), flat).astype(BF)
    er, ec = iotas(size, rows)
    wide = mm(turned, one_hot(ec // per == er)).astype(BF)
    trail_m[...] = jnp.where(r % per == c % per, wide, jnp.zeros_like(wide))
    for h in range(CHUNKS):
        gather_step(h, 1)
    trail_t[...] = trail_m[...].T
    lead_t[...] = lead_m[...].T
    tok_t[...] = tok[...].T
    for h in range(CHUNKS):
        gather_step(h, 2)
    for k in range(CHUNKS):
        settle(ra.at[k, pl.ds(0, others)], a_r.at[k])
        sb[k] = mm(trail_m[...], ra[k]).astype(BF)
        spread(me, n, k, sb, rb, b_s, b_r, piece)
        gather_step(k, 3)
    order_t = natural_order(rows, blocks, per, True)
    for k in range(CHUNKS):
        at = pl.ds(k * cw, cw)
        settle(w.at[k, pl.ds(0, n // 2 * own)], w_r.at[k, 3])
        gate[k] = mm(tok[...], w[k])
        d_mon = (cot[:, at].astype(F32) * gate[k]).astype(BF)
        sc[k] = mm(order_t, d_mon).astype(BF)
        spread(me, n, k, sc, rc, c_s, c_r, piece)
    order = natural_order(rows, blocks, per)
    strip = width // 4
    for k in range(CHUNKS):
        at = pl.ds(k * cw, cw)
        settle(rb.at[k, pl.ds(0, others)], b_r.at[k])
        m = mm(order, rb[k]).astype(BF).astype(F32)
        mixed[:, at] = (m * gate[k]).astype(BF)
        dg[k] = (cot[:, at].astype(F32) * m).astype(BF)
        for q in range(4):
            part[k, q * strip:(q + 1) * strip, :] = mm(
                tok_t[q * strip:(q + 1) * strip, :], dg[k]).astype(BF)
        scatter_step(k, 0)
    swap = inner_first(rows, per)
    for k in range(CHUNKS):
        rb[k] = mm(swap, ra[k]).astype(BF)
    for k in range(CHUNKS):
        scatter_sum(k, 0)
        scatter_step(k, 1)
    for k in range(CHUNKS):
        settle(rc.at[k, pl.ds(0, others)], c_r.at[k])
        sd[k] = mm(trail_t[...], rc[k]).astype(BF)
        spread(me, n, k, sd, rd, d_s, d_r, piece)
    for k in range(CHUNKS):
        back = mm_t(dg[0], w[0, k * cw:(k + 1) * cw, :])
        for h in range(1, CHUNKS):
            back = back + mm_t(dg[h], w[h, k * cw:(k + 1) * cw, :])
        gate[k] = back
    for k in range(CHUNKS):
        scatter_sum(k, 1)
        scatter_step(k, 2)
    for k in range(CHUNKS):
        turned = mm(swap, rc[k]).astype(BF)
        for j in range(per):
            term = mm_t(turned[j * size:(j + 1) * size], rb[k, pl.ds(j * size, size), :])
            g_trail[j] = term if k == 0 else g_trail[j] + term
    for k in range(CHUNKS):
        scatter_sum(k, 2)
        scatter_teams(k)
    for k in range(CHUNKS):
        settle(rd.at[k, pl.ds(0, others)], d_r.at[k])
        d = mm(lead_t[...], rd[k]).astype(BF)
        dcv[k] = d
        hop(dcv.at[k, pl.ds(rows - 16, 16)], hbuf.at[0, k], hs.at[0, k], hr.at[0, k], right)
        hop(dcv.at[k, pl.ds(0, 16)], hbuf.at[1, k], hs.at[1, k], hr.at[1, k], left)
        d = d.astype(F32)
        cp[k] = jnp.concatenate(
            [jnp.sum(d * v, axis=0, keepdims=True) for v in around(k)]
            + [jnp.zeros((5, cw), F32)], axis=0)
        p1[k, mine] = cp[k]
        for t in range(1, group):
            hop(cp.at[k], p1.at[k, mine], p_s.at[k], p_r.at[k],
                team * group + lax.rem(mine + t, group))
        turned = mm(order, rd[k]).astype(BF)
        for a in range(blocks):
            term = mm_t(turned[a * size:(a + 1) * size], conv[k, pl.ds(a * size, size), :])
            g_first[a] = term if k == 0 else g_first[a] + term
    for k in range(CHUNKS):
        settle(p1.at[k, pl.ds(0, group - 1)], p_r.at[k])
        total = p1[k, 0]
        for t in range(1, group):
            total = total + p1[k, t]
        s2[k] = total
        p2[k, team] = total
        for t in range(1, teams):
            hop(s2.at[k], p2.at[k, team], z_s.at[k], z_r.at[k], lax.rem(me + t * group, n))
    for k in range(CHUNKS):
        at = pl.ds(k * cw, cw)
        for side in range(2):
            settle(hbuf.at[side, k], hr.at[side, k])
        before = hbuf[0, k].astype(F32)[15:16]
        after = hbuf[1, k].astype(F32)[0:1]
        before = jnp.where(me == 0, jnp.zeros_like(before), before)
        after = jnp.where(me == n - 1, jnp.zeros_like(after), after)
        d = dcv[k].astype(F32)
        prev, nxt = shifted(d, before, after)
        back = taps[0:1, at] * nxt + taps[1:2, at] * d + taps[2:3, at] * prev
        g_tok[:, at] = (back + gate[k]).astype(BF)
    for k in range(CHUNKS):
        at = pl.ds(k * cw, cw)
        settle(r4.at[k, pl.ds(0, (teams - 1) * own)], g_r.at[k, 3])
        total = r4[k, pl.ds(0, own), :].astype(F32)
        for t in range(1, teams):
            total = total + r4[k, pl.ds(t * own, own), :].astype(F32)
        g_gate[:, at] = total
        settle(p2.at[k, pl.ds(0, teams - 1)], z_r.at[k])
        total = p2[k, 0]
        for t in range(1, teams):
            total = total + p2[k, t]
        g_conv[:, at] = total
    for k in range(CHUNKS):
        settle(halo.at[k], t_s.at[k])
        for buf, sem in ((sa, a_s), (sb, b_s), (sc, c_s), (sd, d_s)):
            settle(buf.at[k, pl.ds(0, others)], sem.at[k])
        for stage in range(4):
            count = (teams - 1) if stage == 0 else teams << (stage - 1)
            settle(w.at[k, pl.ds(0, count * own)], w_s.at[k, stage])
            count = (teams - 1) if stage == 3 else n >> (stage + 1)
            settle(part.at[k, pl.ds(0, count * own)], g_s.at[k, stage])
        settle(p1.at[k, pl.ds(0, group - 1)], p_s.at[k])
        settle(p2.at[k, pl.ds(0, teams - 1)], z_s.at[k])
        for side in range(2):
            settle(hbuf.at[side, k], hs.at[side, k])


def shards(n, tokens, cotangent, taps, gate_weight, lead, trail):
    features, grad_out = tokens[0], cotangent[0]
    rows, width = features.shape
    cw = width // CHUNKS
    own = width // n
    sds = jax.ShapeDtypeStruct
    vmem = pl.BlockSpec(memory_space=pltpu.VMEM)
    dma = pltpu.SemaphoreType.DMA
    block = pltpu.VMEM((CHUNKS, rows, cw), BF)
    square = pltpu.VMEM((rows, rows), BF)
    whole = pltpu.VMEM((CHUNKS, width, cw), BF)

    def pieces(count):
        return pltpu.VMEM((CHUNKS, count * own, cw), BF)

    def tails(count):
        return pltpu.VMEM((CHUNKS, count, 8, cw), F32)

    mixed, grad_tokens, grad_conv, grad_gate, grad_first, grad_trail = pl.pallas_call(
        functools.partial(layer, n),
        out_shape=[sds((rows, width), BF), sds((rows, width), BF), sds((8, width), F32),
                   sds((own, width), F32), sds(lead.shape, F32), sds(trail.shape, F32)],
        in_specs=[vmem] * 6,
        out_specs=[vmem] * 6,
        scratch_shapes=[pltpu.VMEM((2, 16, width), BF), pltpu.VMEM((2, CHUNKS, 16, cw), BF),
                        whole, whole, pieces(n // 2), pieces(n // 4), pieces(n // 8),
                        pieces(n // 8)]
        + [block] * 11
        + [pltpu.VMEM((CHUNKS, rows, cw), F32), pltpu.VMEM((width, rows), BF)]
        + [square] * 4
        + [pltpu.VMEM((CHUNKS, 8, cw), F32), tails(8), pltpu.VMEM((CHUNKS, 8, cw), F32),
           tails(n // 8)]
        + [dma((CHUNKS,))] * 8 + [dma((2,))] * 2 + [dma((2, CHUNKS))] * 2
        + [dma((CHUNKS,))] * 4 + [dma((CHUNKS, 4))] * 4,
        compiler_params=pltpu.CompilerParams(
            collective_id=0, has_side_effects=True, vmem_limit_bytes=LIMIT),
        cost_estimate=pl.CostEstimate(
            flops=12 * rows * width * width, bytes_accessed=10_000_000, transcendentals=0),
        name="layer",
    )(features, grad_out, taps, gate_weight, lead, trail)

    grad_conv, grad_gate, grad_first, grad_trail = lax.psum(
        (grad_conv[:3], grad_gate, grad_first, grad_trail), "dp")
    return mixed[None], grad_tokens[None], grad_conv, grad_gate, grad_first, grad_trail


def solution(mesh):
    seq = P("dp", "seq", None)
    specs = (seq, seq, P(), P("seq", None), P("seq", None, None), P("seq", None, None))
    return jax.shard_map(
        functools.partial(shards, mesh.shape["seq"]),
        mesh=mesh,
        in_specs=specs,
        out_specs=specs,
        check_vma=False,
    )
```

time: 299 us -> 186 us (0.62)
  Pallas kernels: 232 us -> 178 us
  waiting for transfers between devices: 43.5 us -> 0 us
  between operations: 14.1 us -> 0.65 us
    pallas_call x3 -> x1, Pallas kernels: 232 us -> 178 us  [shards(): pl.pallas_call(functools.partial(layer, n), out_shape=[sds((rows, width),...]
    reduce_scatter x1 -> x0, waiting for transfers between devices: 42.8 us -> none  [shards(): grad_gate = lax.psum_scatter(part, 'seq', scatter_dimension=0, tiled=True)]
  transfers between devices with their start and end apart: 2 -> 0, of which waited for: 1 -> 0; matrix products, arithmetic and copies ran while one was open for 0% -> 0% of each run, Pallas kernels for 73% -> 0%
where the time goes in v2:
time: 186 us
  Pallas kernels  178 us (96%)
  local copies, waits for them, and re-layouts  7.46 us (4%)
    pallas_call x1, Pallas kernels, shards(): pl.pallas_call(functools.partial(layer, n), out_shape=[sds((rows, width),...  178 us
    unnamed x13, local copies, waits for them, and re-layouts  6.05 us

profile of v2, /device:TPU:0, one launch (start us, length us, event | category | flops | bytes accessed | tf_op | source)
XLA Modules:
  0.0 186.3 jit_solution(15395415570164356888)
XLA Ops:
  0.6 178.2 %layer.1 = (bf16[512,1536]{1,0:T(8,128)(2,1)}, bf16[512,1536]{1,0:T(8,128)(2,1)}, f32[8,1536]{1,0:T(8,128)}, f32[48,1536]{1,0:T(8,128)}, f32[4,128,128]{2,1,0:T(8,128)}, /*index=5*/f32[4,128,128]{2,1,0:T(8,128)}) custom-call(bf16[512,1536]{1,0:T(8,128)(2,1)} %bitcast.6, bf16[512,1536]{1,0:T(8,128)(2,1)} %bitcast.7, f32[3,1536]{1,0:T(4,128)} %taps.1, ...), custom_call_target="tpu_custom_call" | custom-call | flops 14495514624 | bytes 10000000 | tf_op jit(solution)/shard_map/layer/pallas_call | solution.py:388
  178.8 1.4 slice.3
  180.2 0.0 copy-start
  180.2 2.8 %copy.17 = bf16[1,512,1536]{2,1,0:T(8,128)(2,1)} copy(bf16[1,512,1536]{2,1,0:T(8,128)(2,1)} %bitcast.5) | data formatting | bytes 3145728
  183.0 0.0 copy-done
  183.0 0.0 copy-start.1
  183.0 0.0 copy-start.3
  183.0 0.0 copy-start.2
  183.0 1.1 copy.18
  184.2 0.0 copy-done.1
  184.2 0.7 copy.19
  184.9 0.0 copy-done.3
  184.9 0.7 copy.20
  185.6 0.0 copy-done.2
  185.6 0.7 copy.21
Async XLA Ops:
  180.2 2.8 %copy-start = (bf16[512,1536]{1,0:T(8,128)(2,1)S(1)}, bf16[512,1536]{1,0:T(8,128)(2,1)}, u32[]{:S(2)}) copy-start(bf16[512,1536]{1,0:T(8,128)(2,1)} %get-tuple-element.13) | copy-start | bytes 4718596
  183.0 1.2 copy-start.1
  183.0 1.9 %copy-start.3 = (f32[4,128,128]{2,1,0:T(8,128)S(1)}, f32[4,128,128]{2,1,0:T(8,128)}, u32[]{:S(2)}) copy-start(f32[4,128,128]{2,1,0:T(8,128)} %get-tuple-element.28) | copy-start | bytes 786436
  183.0 2.6 %copy-start.2 = (f32[4,128,128]{2,1,0:T(8,128)S(1)}, f32[4,128,128]{2,1,0:T(8,128)}, u32[]{:S(2)}) copy-start(f32[4,128,128]{2,1,0:T(8,128)} %get-tuple-element.29) | copy-start | bytes 786436

commit v3 on v2

--- a/solution.py
+++ b/solution.py
@@ -58,7 +58,7 @@
         return carry
 
     lax.fori_loop(1, n, body, 0)
-    pl.semaphore_wait(barrier, n - 1)
+    return barrier
 
 
 def spread(me, n, k, src, dst, send_sem, recv_sem, piece):
@@ -117,12 +117,12 @@
 
 
 def layer(
-    n, tok, cot, taps, gw, lead, trail,
-    mixed, g_tok, g_conv, g_gate, g_first, g_trail,
-    halo, hbuf, w, part, r1, r2, r3, r4, conv, sa, ra, sb, rb, sc, rc, sd, rd, dcv, dg, gate,
+    n, tok, cot_in, taps, gw, lead, trail,
+    mixed_out, g_tok_out, g_conv, g_gate, g_first, g_trail,
+    cot, mixed, g_tok, halo, hbuf, w, part, r1, r2, r3, r4, conv, sa, ra, sb, rb, sc, rc, sd, rd, dcv, dg, gate,
     tok_t, lead_m, lead_t, trail_m, trail_t, cp, p1, s2, p2,
     a_s, a_r, b_s, b_r, c_s, c_r, d_s, d_r, t_s, t_r, hs, hr, p_s, p_r, z_s, z_r,
-    w_s, w_r, g_s, g_r,
+    w_s, w_r, g_s, g_r, in_s, m_s, o_s,
 ):
     me = lax.axis_index("seq")
     right, left = lax.rem(me + 1, n), lax.rem(me + n - 1, n)
@@ -210,32 +210,58 @@
             hop(part.at[h, band(peer, own)], r4.at[h, band(team, own)], g_s.at[h, 3],
                 g_r.at[h, 3], peer)
 
-    greet(me, n)
-    hop(tok.at[pl.ds(rows - 16, 16)], halo.at[0], t_s.at[0], t_r.at[0], right)
-    hop(tok.at[pl.ds(0, 16)], halo.at[1], t_s.at[1], t_r.at[1], left)
-    gather_teams()
+    def leaving(src, dst, k, sem):
+        at = pl.ds(k * cw, cw)
+        return pltpu.make_async_copy(src.at[:, at], dst.at[:, at], sem.at[k])
+
+    barrier = greet(me, n)
+    fetch = pltpu.make_async_copy(cot_in, cot, in_s.at[0])
+    fetch.start()
     r, c = iotas(rows, rows)
     flat = jnp.concatenate([lead[a] for a in range(blocks)], axis=0)
     turned = mm(natural_order(rows, blocks, per, True), flat).astype(BF)
     wide = jnp.concatenate([turned] * blocks, axis=1)
     lead_m[...] = jnp.where((r // per) % blocks == c // size, wide, jnp.zeros_like(wide))
+
+    def taps_over(at, prev, x, nxt):
+        return (taps[0:1, at] * prev + taps[1:2, at] * x + taps[2:3, at] * nxt).astype(BF)
+
+    for k in range(CHUNKS):
+        at = pl.ds(k * cw, cw)
+        x = tok[:, at].astype(F32)
+        none = jnp.zeros((1, cw), F32)
+        prev, nxt = shifted(x, none, none)
+        conv[k] = taps_over(at, prev, x, nxt)
+    pl.semaphore_wait(barrier, n - 1)
+    hop(tok.at[pl.ds(rows - 16, 16)], halo.at[0], t_s.at[0], t_r.at[0], right)
+    hop(tok.at[pl.ds(0, 16)], halo.at[1], t_s.at[1], t_r.at[1], left)
+    gather_teams()
     for side in range(2):
         settle(halo.at[side], t_r.at[side])
 
-    def around(k):
-        at = pl.ds(k * cw, cw)
-        x = tok[:, at].astype(F32)
+    def sides(k):
+        at = pl.ds(k * cw, cw)
         before = halo[0, :, at].astype(F32)[15:16]
         after = halo[1, :, at].astype(F32)[0:1]
         before = jnp.where(me == 0, jnp.zeros_like(before), before)
         after = jnp.where(me == n - 1, jnp.zeros_like(after), after)
-        prev, nxt = shifted(x, before, after)
+        return before, after
+
+    def around(k):
+        at = pl.ds(k * cw, cw)
+        x = tok[:, at].astype(F32)
+        prev, nxt = shifted(x, *sides(k))
         return prev, x, nxt
 
     for k in range(CHUNKS):
         at = pl.ds(k * cw, cw)
-        prev, x, nxt = around(k)
-        conv[k] = (taps[0:1, at] * prev + taps[1:2, at] * x + taps[2:3, at] * nxt).astype(BF)
+        edge = lax.broadcasted_iota(jnp.int32, (16, cw), 0)
+        for first, row in ((0, 0), (rows - 16, 15)):
+            slab = pl.ds(first, 16)
+            x = tok[slab, at].astype(F32)
+            prev, nxt = shifted(x, *sides(k))
+            fixed = taps_over(at, prev, x, nxt).astype(F32)
+            conv[k, slab, :] = jnp.where(edge == row, fixed, conv[k, slab, :].astype(F32)).astype(BF)
         sa[k] = mm(lead_m[...], conv[k]).astype(BF)
         spread(me, n, k, sa, ra, a_s, a_r, piece)
     flat = jnp.concatenate([trail[j] for j in range(per)], axis=0)
@@ -256,6 +282,7 @@
         spread(me, n, k, sb, rb, b_s, b_r, piece)
         gather_step(k, 3)
     order_t = natural_order(rows, blocks, per, True)
+    fetch.wait()
     for k in range(CHUNKS):
         at = pl.ds(k * cw, cw)
         settle(w.at[k, pl.ds(0, n // 2 * own)], w_r.at[k, 3])
@@ -270,6 +297,7 @@
         settle(rb.at[k, pl.ds(0, others)], b_r.at[k])
         m = mm(order, rb[k]).astype(BF).astype(F32)
         mixed[:, at] = (m * gate[k]).astype(BF)
+        leaving(mixed, mixed_out, k, m_s).start()
         dg[k] = (cot[:, at].astype(F32) * m).astype(BF)
         for q in range(4):
             part[k, q * strip:(q + 1) * strip, :] = mm(
@@ -279,12 +307,13 @@
     for k in range(CHUNKS):
         rb[k] = mm(swap, ra[k]).astype(BF)
     for k in range(CHUNKS):
-        scatter_sum(k, 0)
-        scatter_step(k, 1)
-    for k in range(CHUNKS):
         settle(rc.at[k, pl.ds(0, others)], c_r.at[k])
         sd[k] = mm(trail_t[...], rc[k]).astype(BF)
         spread(me, n, k, sd, rd, d_s, d_r, piece)
+        if k == 0:
+            for h in range(CHUNKS):
+                scatter_sum(h, 0)
+                scatter_step(h, 1)
     for k in range(CHUNKS):
         back = mm_t(dg[0], w[0, k * cw:(k + 1) * cw, :])
         for h in range(1, CHUNKS):
@@ -340,6 +369,7 @@
         prev, nxt = shifted(d, before, after)
         back = taps[0:1, at] * nxt + taps[1:2, at] * d + taps[2:3, at] * prev
         g_tok[:, at] = (back + gate[k]).astype(BF)
+        leaving(g_tok, g_tok_out, k, o_s).start()
     for k in range(CHUNKS):
         at = pl.ds(k * cw, cw)
         settle(r4.at[k, pl.ds(0, (teams - 1) * own)], g_r.at[k, 3])
@@ -351,9 +381,12 @@
         total = p2[k, 0]
         for t in range(1, teams):
             total = total + p2[k, t]
-        g_conv[:, at] = total
-    for k in range(CHUNKS):
-        settle(halo.at[k], t_s.at[k])
+        g_conv[:, at] = total[0:3]
+    for side in range(2):
+        settle(halo.at[side], t_s.at[side])
+    for k in range(CHUNKS):
+        leaving(mixed, mixed_out, k, m_s).wait()
+        leaving(g_tok, g_tok_out, k, o_s).wait()
         for buf, sem in ((sa, a_s), (sb, b_s), (sc, c_s), (sd, d_s)):
             settle(buf.at[k, pl.ds(0, others)], sem.at[k])
         for stage in range(4):
@@ -367,6 +400,24 @@
             settle(hbuf.at[side, k], hs.at[side, k])
 
 
+CUTS = (4, 4, 1, 1, 1, 1)
+
+
+def handed_on(*refs):
+    count = len(CUTS)
+    srcs, dsts, sem = refs[:count], refs[count:2 * count], refs[-1]
+    copies = []
+    for cuts, src, dst in zip(CUTS, srcs, dsts):
+        step = src.shape[0] // cuts
+        for q in range(cuts):
+            at = pl.ds(q * step, step)
+            copies.append(pltpu.make_async_copy(src.at[at], dst.at[at], sem.at[len(copies)]))
+    for copy in copies:
+        copy.start()
+    for copy in copies:
+        copy.wait()
+
+
 def shards(n, tokens, cotangent, taps, gate_weight, lead, trail):
     features, grad_out = tokens[0], cotangent[0]
     rows, width = features.shape
@@ -385,13 +436,15 @@
     def tails(count):
         return pltpu.VMEM((CHUNKS, count, 8, cw), F32)
 
-    mixed, grad_tokens, grad_conv, grad_gate, grad_first, grad_trail = pl.pallas_call(
+    anywhere = pl.BlockSpec(memory_space=pl.ANY)
+    shapes = [sds((rows, width), BF), sds((rows, width), BF), sds((3, width), F32),
+              sds((own, width), F32), sds(lead.shape, F32), sds(trail.shape, F32)]
+    results = pl.pallas_call(
         functools.partial(layer, n),
-        out_shape=[sds((rows, width), BF), sds((rows, width), BF), sds((8, width), F32),
-                   sds((own, width), F32), sds(lead.shape, F32), sds(trail.shape, F32)],
-        in_specs=[vmem] * 6,
-        out_specs=[vmem] * 6,
-        scratch_shapes=[pltpu.VMEM((2, 16, width), BF), pltpu.VMEM((2, CHUNKS, 16, cw), BF),
+        out_shape=shapes,
+        in_specs=[vmem, anywhere] + [vmem] * 4,
+        out_specs=[anywhere] * 2 + [vmem] * 4,
+        scratch_shapes=[pltpu.VMEM((rows, width), BF)] * 3 + [pltpu.VMEM((2, 16, width), BF), pltpu.VMEM((2, CHUNKS, 16, cw), BF),
                         whole, whole, pieces(n // 2), pieces(n // 4), pieces(n // 8),
                         pieces(n // 8)]
         + [block] * 11
@@ -400,7 +453,7 @@
         + [pltpu.VMEM((CHUNKS, 8, cw), F32), tails(8), pltpu.VMEM((CHUNKS, 8, cw), F32),
            tails(n // 8)]
         + [dma((CHUNKS,))] * 8 + [dma((2,))] * 2 + [dma((2, CHUNKS))] * 2
-        + [dma((CHUNKS,))] * 4 + [dma((CHUNKS, 4))] * 4,
+        + [dma((CHUNKS,))] * 4 + [dma((CHUNKS, 4))] * 4 + [dma((1,)), dma((CHUNKS,)), dma((CHUNKS,))],
         compiler_params=pltpu.CompilerParams(
             collective_id=0, has_side_effects=True, vmem_limit_bytes=LIMIT),
         cost_estimate=pl.CostEstimate(
@@ -408,8 +461,18 @@
         name="layer",
     )(features, grad_out, taps, gate_weight, lead, trail)
 
+    mixed, grad_tokens, grad_conv, grad_gate, grad_first, grad_trail = pl.pallas_call(
+        handed_on,
+        out_shape=shapes,
+        in_specs=[anywhere] * 6,
+        out_specs=[anywhere] * 6,
+        scratch_shapes=[dma((sum(CUTS),))],
+        compiler_params=pltpu.CompilerParams(vmem_limit_bytes=LIMIT),
+        name="handed_on",
+    )(*results)
+
     grad_conv, grad_gate, grad_first, grad_trail = lax.psum(
-        (grad_conv[:3], grad_gate, grad_first, grad_trail), "dp")
+        (grad_conv, grad_gate, grad_first, grad_trail), "dp")
     return mixed[None], grad_tokens[None], grad_conv, grad_gate, grad_first, grad_trail
 
 

time: 186 us -> 300 us (1.61)
  Pallas kernels: 178 us -> 299 us
  local copies, waits for them, and re-layouts: 7.46 us -> 0 us
    pallas_call x1 -> x2, Pallas kernels: 178 us -> 299 us  [the longest x1 177 us: shards(): pl.pallas_call(functools.partial(layer, n), out_shape=shapes, in_specs=[v...]
    unnamed x13 -> x0, local copies, waits for them, and re-layouts: 6.05 us -> none
where the time goes in v3:
time: 300 us
  Pallas kernels  299 us (100%)
    pallas_call x1, Pallas kernels, shards(): pl.pallas_call(functools.partial(layer, n), out_shape=shapes, in_specs=[v...  177 us
    pallas_call x1, Pallas kernels, shards(): pl.pallas_call(handed_on, out_shape=shapes, in_specs=[anywhere] * 6, out_...  122 us

profile of v3, /device:TPU:0, one launch (start us, length us, event | category | flops | bytes accessed | tf_op | source)
XLA Modules:
  0.0 299.7 jit_solution(14541890246921873010)
XLA Ops:
  0.6 176.8 %layer.1 = (bf16[512,1536]{1,0:T(8,128)(2,1)}, bf16[512,1536]{1,0:T(8,128)(2,1)}, f32[3,1536]{1,0:T(4,128)}, f32[48,1536]{1,0:T(8,128)}, f32[4,128,128]{2,1,0:T(8,128)}, /*index=5*/f32[4,128,128]{2,1,0:T(8,128)}) custom-call(bf16[512,1536]{1,0:T(8,128)(2,1)} %bitcast.4, bf16[512,1536]{1,0:T(8,128)(2,1)} %bitcast.5, f32[3,1536]{1,0:T(4,128)} %taps.1, ...), custom_call_target="tpu_custom_call" | custom-call | flops 14495514624 | bytes 10000000 | tf_op jit(solution)/shard_map/layer/pallas_call | solution.py:442
  177.5 122.1 %handed_on.1 = (bf16[512,1536]{1,0:T(8,128)(2,1)}, bf16[512,1536]{1,0:T(8,128)(2,1)}, f32[3,1536]{1,0:T(4,128)}, f32[48,1536]{1,0:T(8,128)}, f32[4,128,128]{2,1,0:T(8,128)}, /*index=5*/f32[4,128,128]{2,1,0:T(8,128)}) custom-call(bf16[512,1536]{1,0:T(8,128)(2,1)} %get-tuple-element.18.refs_0_, bf16[512,1536]{1,0:T(8,128)(2,1)} %get-tuple-element.19.refs_1_, ...), custom_call_target="tpu_custom_call" | custom-call | tf_op jit(solution)/shard_map/handed_on/pallas_call | solution.py:464

commit v4 on v3

--- a/solution.py
+++ b/solution.py
@@ -400,22 +400,10 @@
             settle(hbuf.at[side, k], hs.at[side, k])
 
 
-CUTS = (4, 4, 1, 1, 1, 1)
-
-
 def handed_on(*refs):
-    count = len(CUTS)
-    srcs, dsts, sem = refs[:count], refs[count:2 * count], refs[-1]
-    copies = []
-    for cuts, src, dst in zip(CUTS, srcs, dsts):
-        step = src.shape[0] // cuts
-        for q in range(cuts):
-            at = pl.ds(q * step, step)
-            copies.append(pltpu.make_async_copy(src.at[at], dst.at[at], sem.at[len(copies)]))
-    for copy in copies:
-        copy.start()
-    for copy in copies:
-        copy.wait()
+    half = len(refs) // 2
+    for src, dst in zip(refs[:half], refs[half:]):
+        dst[...] = src[...]
 
 
 def shards(n, tokens, cotangent, taps, gate_weight, lead, trail):
@@ -461,12 +449,19 @@
         name="layer",
     )(features, grad_out, taps, gate_weight, lead, trail)
 
+    steps = lead.shape[0]
+    rows_of = pl.BlockSpec((rows // steps, width), lambda i: (i, 0))
+    same = pl.BlockSpec((3, width), lambda i: (0, 0))
+    all_own = pl.BlockSpec((own, width), lambda i: (0, 0))
+    lead_of = pl.BlockSpec((1,) + lead.shape[1:], lambda i: (i, 0, 0))
+    trail_of = pl.BlockSpec((trail.shape[0] // steps,) + trail.shape[1:], lambda i: (i, 0, 0))
+    tiles = [rows_of, rows_of, same, all_own, lead_of, trail_of]
     mixed, grad_tokens, grad_conv, grad_gate, grad_first, grad_trail = pl.pallas_call(
         handed_on,
+        grid=(steps,),
         out_shape=shapes,
-        in_specs=[anywhere] * 6,
-        out_specs=[anywhere] * 6,
-        scratch_shapes=[dma((sum(CUTS),))],
+        in_specs=tiles,
+        out_specs=tiles,
         compiler_params=pltpu.CompilerParams(vmem_limit_bytes=LIMIT),
         name="handed_on",
     )(*results)

time: 300 us -> 183 us (0.61)
  Pallas kernels: 299 us -> 182 us
    pallas_call x1, Pallas kernels: 122 us -> 4.79 us  [shards(): pl.pallas_call(handed_on, grid=(steps,), out_shape=shapes, in_specs=tiles...]
where the time goes in v4:
time: 183 us; the launch traced here: 182 us
  Pallas kernels  182 us (99%)
    pallas_call x1, Pallas kernels, shards(): pl.pallas_call(functools.partial(layer, n), out_shape=shapes, in_specs=[v...  177 us
    pallas_call x1, Pallas kernels, shards(): pl.pallas_call(handed_on, grid=(steps,), out_shape=shapes, in_specs=tiles...  4.79 us

profile of v4, /device:TPU:0, one launch (start us, length us, event | category | flops | bytes accessed | tf_op | source)
XLA Modules:
  0.0 182.4 jit_solution(15027874293910493950)
XLA Ops:
  0.6 176.8 %layer.1 = (bf16[512,1536]{1,0:T(8,128)(2,1)}, bf16[512,1536]{1,0:T(8,128)(2,1)}, f32[3,1536]{1,0:T(4,128)}, f32[48,1536]{1,0:T(8,128)}, f32[4,128,128]{2,1,0:T(8,128)}, /*index=5*/f32[4,128,128]{2,1,0:T(8,128)}) custom-call(bf16[512,1536]{1,0:T(8,128)(2,1)} %bitcast.4, bf16[512,1536]{1,0:T(8,128)(2,1)} %bitcast.5, f32[3,1536]{1,0:T(4,128)} %taps.1, ...), custom_call_target="tpu_custom_call" | custom-call | flops 14495514624 | bytes 10000000 | tf_op jit(solution)/shard_map/layer/pallas_call | solution.py:430
  177.5 4.8 %handed_on.1 = (bf16[512,1536]{1,0:T(8,128)(2,1)}, bf16[512,1536]{1,0:T(8,128)(2,1)}, f32[3,1536]{1,0:T(4,128)}, f32[48,1536]{1,0:T(8,128)}, f32[4,128,128]{2,1,0:T(8,128)}, /*index=5*/f32[4,128,128]{2,1,0:T(8,128)}) custom-call(bf16[512,1536]{1,0:T(8,128)(2,1)} %get-tuple-element.18.refs_0_, bf16[512,1536]{1,0:T(8,128)(2,1)} %get-tuple-element.19.refs_1_, ...), custom_call_target="tpu_custom_call" | custom-call | tf_op jit(solution)/shard_map/handed_on/pallas_call | solution.py:459
